TPU v7x, 512 devices: a whole 4x4x16 slice. The times are simulated.
512 devices in a mesh: dp: 32 (over y, x, core), tm: 16 (over z).
Axes of the slice: x: 4, y: 4, z: 16, core: 2. Of those that a mesh axis runs over, the one named last changes fastest.
Arguments:
- phonemes: bfloat16 [32, 256, 1024], P('dp', 'tm'), may hold values from -6 to 6
- durations: int32 [32, 256], P('dp', 'tm'), may hold values from 1 to 32, 2048 in all within a row
- conv_weight: bfloat16 [9, 1024, 2048], P(None, None, 'tm'), may hold values from -0.0625 to 0.0625
- out_weight: bfloat16 [2048, 1024], P('tm', 'dp'), may hold values from -0.125 to 0.125
- norm_gain: float32 [1024], replicated, may hold values from 0.1 to 1.9
Outputs:
- decoded: bfloat16 [32, 2048, 1024], P('dp', 'tm')
Inputs may be any that keep to these rules, and one draw needn't show every extreme that they name: Each utterance's durations sum to 2048, and in each utterance some phoneme lasts exactly 32 frames.
All inputs are finite; a program needn't handle non-finite values. No bound on the sum of `durations` on one device may be relied on, other than what follows from the above.
Results may differ from a plain program's by a relative error of at most 0.015.
Values may be sent and summed in bfloat16 or wider, within the bound.
A program may use at most 64 MiB of HBM per device.

v0:
```python
import jax
import jax.numpy as jnp
from jax import lax
from jax.sharding import PartitionSpec as P

KER = 9
FR = 128


def on_device(phonemes, durations, conv_weight, out_weight, norm_gain):
    margin = KER // 2
    rows_all, lengths_all = (
        lax.all_gather(phonemes, "tm", axis=1, tiled=True),
        lax.all_gather(durations, "tm", axis=1, tiled=True),
    )
    rows_all = rows_all[0]
    phone_lengths = lengths_all[0]
    phone_ends = jnp.cumsum(phone_lengths).astype(jnp.int32)
    phone_starts = phone_ends - phone_lengths
    total_frames = FR * lax.axis_size("tm")
    first_own = lax.axis_index("tm") * FR
    positions = first_own + jnp.arange(FR, dtype=jnp.int32)
    inside = (positions[:, None] >= phone_starts[None, :]) & (
        positions[:, None] < phone_ends[None, :]
    )
    own_rows = jnp.dot(
        inside.astype(jnp.bfloat16), rows_all, preferred_element_type=jnp.float32
    ).astype(jnp.bfloat16)
    frames = lax.all_gather(own_rows, "tm", axis=0, tiled=True)
    padded = jnp.pad(frames, ((margin, margin), (0, 0)))
    pre_act = jnp.zeros((total_frames, conv_weight.shape[2]), jnp.float32)
    for offset in range(KER):
        pre_act = pre_act + jnp.dot(
            padded[offset : offset + total_frames],
            conv_weight[offset],
            preferred_element_type=jnp.float32,
        )
    hidden = jnp.maximum(pre_act, 0.0).astype(jnp.bfloat16)
    columns = lax.all_gather(out_weight, "dp", axis=1, tiled=True)
    reduced = lax.psum_scatter(
        jnp.dot(hidden, columns, preferred_element_type=jnp.float32).astype(jnp.bfloat16),
        "tm",
        scatter_dimension=0,
        tiled=True,
    ).astype(jnp.float32)
    summed = own_rows.astype(jnp.float32) + reduced
    average = jnp.mean(summed, axis=-1, keepdims=True)
    centered = summed - average
    spread = jnp.mean(centered * centered, axis=-1, keepdims=True)
    decoded = centered * lax.rsqrt(spread + 1e-05) * norm_gain
    return decoded.astype(jnp.bfloat16)[None]


def solution(mesh):
    placed = (P("dp", "tm", None), P("dp", "tm"), P(None, None, "tm"), P("tm", "dp"), P())
    return jax.shard_map(
        on_device, mesh=mesh, in_specs=placed, out_specs=P("dp", "tm", None), check_vma=False
    )
```

profile of v0, /device:TPU:2, one launch (start us, length us, event | category | flops | bytes accessed | tf_op | source)
XLA Modules:
  0.0 252.1 jit_solution(1046039252529930426)
XLA Ops:
  6.5 1.3 dynamic-slice
  8.5 0.8 bitcast_dynamic-update-slice_fusion
  9.2 26.7 %all-reduce.1 = s32[256]{0:T(256)S(1)} all-reduce(s32[256]{0:T(256)S(1)} %bitcast_dynamic-update-slice_fusion), channel_id=1, replica_groups=mesh['dp'=32,'tm'=16] {'tm'}, use_global_device_ids=true, to_apply=%add.1 | all-reduce | flops 256 | bytes 2048
  35.9 0.3 reduce-window.9
  36.2 0.1 slice.59
  36.3 0.1 slice_reduce_fusion
  36.5 0.1 fusion.91
  36.6 30.0 %all_gather.13 = bf16[1,256,1024]{2,1,0:T(8,128)(2,1)S(1)} all-gather(bf16[1,16,1024]{2,1,0:T(8,128)(2,1)} %param.5), channel_id=1, replica_groups=mesh['dp'=32,'tm'=16] {'tm'}, dimensions={1}, use_global_device_ids=true | all-gather | bytes 557056 | tf_op jit(solution)/shard_map/all_gather | solution.py:13
  66.6 1.0 convolution_convert_fusion.1
  67.6 24.8 %all_gather.15 = bf16[128,1024]{0,1:T(8,128)(2,1)S(1)} all-gather(bf16[128,32]{0,1:T(8,128)(2,1)} %param.8), channel_id=1, replica_groups=mesh['dp'=32,'tm'=16] {'dp'}, dimensions={1}, use_global_device_ids=true | all-gather | bytes 270336 | tf_op jit(solution)/shard_map/all_gather | solution.py:39
  92.4 51.4 %all-gather.2.cloned.1.call-done = bf16[2048,1024]{1,0:T(8,128)(2,1)} async-done(((bf16[128,1024]{1,0:T(8,128)(2,1)}), bf16[2048,1024]{1,0:T(8,128)(2,1)}) %all-gather.2.cloned.1.call-update) | async-done | bytes 4194320 | tf_op jit(solution)/shard_map/all_gather | solution.py:29
  143.8 3.6 %fusion.12 = f32[2048,128]{1,0:T(8,128)S(1)} fusion(bf16[2048,1024]{1,0:T(8,128)(2,1)} %all-gather.2.cloned.1.call-done, bf16[9,1024,128]{2,1,0:T(8,128)(2,1)} %param.7), kind=kOutput, calls=%fused_computation.12 | convolution fusion | flops 536870912 | bytes 5505024 | tf_op jit(solution)/shard_map/dot_general | solution.py:33
  147.5 1.3 fusion.10
  148.8 1.3 fusion.6
  150.1 1.3 fusion.4
  151.3 1.3 fusion.2
  152.6 1.3 fusion.22
  154.0 1.3 fusion.25
  155.2 2.3 fusion.18
  157.6 6.8 %convolution_convert_fusion = bf16[2048,1024]{1,0:T(8,128)(2,1)} fusion(bf16[128,1024]{0,1:T(8,128)(2,1)S(1)} %all_gather.15, f32[2048,128]{1,0:T(8,128)S(1)} %fusion.18, bf16[2048,1024]{1,0:T(8,128)(2,1)} %all-gather.2.cloned.1.call-done, bf16[9,1024,128]{2,1,0:T(8,128)(2,1)} %param.7), kind=kOutput, calls=%fused_computation.16 | convolution fusion | flops 1076625408 | bytes 9961472 | tf_op jit(solution)/shard_map/dot_general | solution.py:41
  164.3 76.8 %reduce-scatter.2.cloned.1.call-done = bf16[128,1024]{1,0:T(8,128)(2,1)} async-done(((bf16[2048,1024]{1,0:T(8,128)(2,1)}), bf16[128,1024]{1,0:T(8,128)(2,1)}) %reduce-scatter.2.cloned.1.call-update) | async-done | bytes 262160 | tf_op jit(solution)/shard_map/reduce_scatter | solution.py:40
  241.2 1.1 fusion.51
  242.3 1.2 multiply_reduce_fusion
  243.4 1.8 fusion.52
  (19 shorter events, 0.2 us)
Async XLA Ops:
  6.5 137.3 %all-gather.2.cloned.1.call-start = ((), (), s32[]{:S(2)}) async-start(), calls=%async_computation.1 | async-start | bytes 4456448 | tf_op jit(solution)/shard_map/all_gather | solution.py:29
  67.6 173.6 %reduce-scatter.2.cloned.1.call-start = ((), (), s32[]{:S(2)}) async-start(), calls=%async_computation.2 | async-start | bytes 4456448 | tf_op jit(solution)/shard_map/reduce_scatter | solution.py:40
  92.4 55.1 %copy-start.2 = (bf16[9,1024,128]{2,1,0:T(8,128)(2,1)S(1)}, bf16[9,1024,128]{2,1,0:T(8,128)(2,1)}, u32[]{:S(2)}) copy-start(bf16[9,1024,128]{2,1,0:T(8,128)(2,1)} %param.7) | copy-start | bytes 7077892
  143.8 3.7 %copy-start = (bf16[2048,1024]{1,0:T(8,128)(2,1)S(1)}, bf16[2048,1024]{1,0:T(8,128)(2,1)}, u32[]{:S(2)}) copy-start(bf16[2048,1024]{1,0:T(8,128)(2,1)} %all-gather.2.cloned.1.call-done) | copy-start | bytes 12582916
  164.3 76.8 %copy-start.1 = (bf16[128,1024]{1,0:T(8,128)(2,1)S(1)}, bf16[128,1024]{1,0:T(8,128)(2,1)}, u32[]{:S(2)}) copy-start(bf16[128,1024]{1,0:T(8,128)(2,1)} %convolution_convert_fusion.1) | copy-start | bytes 786436
  164.3 79.1 %copy-start.3 = (f32[1024]{0:T(1024)S(1)}, f32[1024]{0:T(1024)}, u32[]{:S(2)}) copy-start(f32[1024]{0:T(1024)} %param.9) | copy-start | bytes 12292
Sparse Core Ops, SparseCore 0:
  67.7 76.0 all-gather.1
  164.5 76.6 reduce-scatter.1
where the time goes:
time: 252 us
  waiting for transfers between devices  128 us (51%)
  blocking collectives  81.5 us (32%)
  matrix products  21.4 us (8%)
  between operations  14.1 us (6%)
  other arithmetic  4.56 us (2%)
    reduce_scatter x1, waiting for transfers between devices, on_device(): lax.psum_scatter(jnp.dot(hidden, columns, preferred_element_type=jnp.floa...  76.8 us
    all_gather x1, waiting for transfers between devices, on_device(): frames = lax.all_gather(own_rows, 'tm', axis=0, tiled=True)  51.4 us
    all_gather x1, blocking collectives, on_device(): lax.all_gather(phonemes, 'tm', axis=1, tiled=True)  30 us
    unnamed x1, blocking collectives  26.7 us
    all_gather x1, blocking collectives, on_device(): columns = lax.all_gather(out_weight, 'dp', axis=1, tiled=True)  24.8 us
    dot_general x8, matrix products, on_device(): jnp.dot(padded[offset:offset + total_frames], conv_weight[offset], prefer...  13.7 us
    dot_general x1, matrix products, on_device(): jnp.dot(hidden, columns, preferred_element_type=jnp.float32)  6.75 us
  transfers between devices with their start and end apart: 2, of which 2 were waited for; matrix products, arithmetic and copies ran while one was open for 0% of the time, Pallas kernels for 0%

commit v1 on v0

--- a/solution.py
+++ b/solution.py
@@ -5,6 +5,27 @@
 
 KER = 9
 FR = 128
+
+
+def collect(x, axis, dim):
+    size, here, span = (lax.axis_size(axis), lax.axis_index(axis), x.shape[dim])
+    upward = [(i, (i + 1) % size) for i in range(size)]
+    behind = [(i, (i - 1) % size) for i in range(size)]
+    whole = jnp.zeros((*x.shape[:dim], size * span, *x.shape[dim + 1 :]), x.dtype)
+    whole = lax.dynamic_update_slice_in_dim(whole, x, here * span, axis=dim)
+    from_left = from_right = x
+    half = size // 2
+    for step in range(1, half + 1):
+        from_left = lax.ppermute(from_left, axis, upward)
+        whole = lax.dynamic_update_slice_in_dim(
+            whole, from_left, (here - step) % size * span, axis=dim
+        )
+        if step < size - half:
+            from_right = lax.ppermute(from_right, axis, behind)
+            whole = lax.dynamic_update_slice_in_dim(
+                whole, from_right, (here + step) % size * span, axis=dim
+            )
+    return whole
 
 
 def on_device(phonemes, durations, conv_weight, out_weight, norm_gain):
@@ -26,7 +47,7 @@
     own_rows = jnp.dot(
         inside.astype(jnp.bfloat16), rows_all, preferred_element_type=jnp.float32
     ).astype(jnp.bfloat16)
-    frames = lax.all_gather(own_rows, "tm", axis=0, tiled=True)
+    frames = collect(own_rows, "tm", 0)
     padded = jnp.pad(frames, ((margin, margin), (0, 0)))
     pre_act = jnp.zeros((total_frames, conv_weight.shape[2]), jnp.float32)
     for offset in range(KER):

time: 252 us -> 305 us (1.21)
  the two profiles are of different devices: /device:TPU:2 before, /device:TPU:6 now
where the time goes in v1:
time: 305 us; the launch traced here: 304 us
  waiting for transfers between devices  92.1 us (30%)
  blocking collectives  81.8 us (27%)
  starting transfers between devices  52.9 us (17%)
  matrix products  43.3 us (14%)
  local copies, waits for them, and re-layouts  15.7 us (5%)
  between operations  14.2 us (5%)
  other arithmetic  4.56 us (1%)
    reduce_scatter x1, waiting for transfers between devices, on_device(): lax.psum_scatter(jnp.dot(hidden, columns, preferred_element_type=jnp.floa...  75.6 us
    ppermute x7, starting transfers between devices, collect(): from_right = lax.ppermute(from_right, axis, behind)  36.3 us
    dot_general x8, matrix products, on_device(): jnp.dot(padded[offset:offset + total_frames], conv_weight[offset], prefer...  33.7 us
    all_gather x1, blocking collectives, on_device(): lax.all_gather(phonemes, 'tm', axis=1, tiled=True)  30.3 us
    unnamed x1, blocking collectives  26.7 us
    all_gather x1, blocking collectives, on_device(): columns = lax.all_gather(out_weight, 'dp', axis=1, tiled=True)  24.8 us
    ppermute x8, starting transfers between devices, collect(): from_left = lax.ppermute(from_left, axis, upward)  16.5 us
    ppermute x8, waiting for transfers between devices, collect(): from_left = lax.ppermute(from_left, axis, upward)  12.4 us
  transfers between devices with their start and end apart: 16, of which 8 were waited for; matrix products, arithmetic and copies ran while one was open for 3% of the time, Pallas kernels for 0%

profile of v1, /device:TPU:6, one launch (start us, length us, event | category | flops | bytes accessed | tf_op | source)
XLA Modules:
  0.0 304.4 jit_solution(15041255984495190238)
XLA Ops:
  9.2 26.7 %all-reduce.1 = s32[256]{0:T(256)S(1)} all-reduce(s32[256]{0:T(256)S(1)} %bitcast_dynamic-update-slice_fusion), channel_id=1, replica_groups=mesh['dp'=32,'tm'=16] {'tm'}, use_global_device_ids=true, to_apply=%add.1 | all-reduce | flops 256 | bytes 2048
  36.6 30.3 %all_gather.10 = bf16[1,256,1024]{2,1,0:T(8,128)(2,1)S(1)} all-gather(bf16[1,16,1024]{2,1,0:T(8,128)(2,1)} %param.5), channel_id=1, replica_groups=mesh['dp'=32,'tm'=16] {'tm'}, dimensions={1}, use_global_device_ids=true | all-gather | bytes 557056 | tf_op jit(solution)/shard_map/all_gather | solution.py:34
  67.0 2.5 broadcast_in_dim.4
  70.4 3.0 collective-permute-start
  73.4 4.0 %collective-permute-start.1 = (bf16[128,1024]{1,0:T(8,128)(2,1)S(1)}, bf16[128,1024]{1,0:T(8,128)(2,1)S(1)}, u32[]{:S(2)}, u32[]{:S(2)}) collective-permute-start(bf16[128,1024]{1,0:T(8,128)(2,1)S(1)} %get-tuple-element.6), channel_id=1, source_target_pairs={{0,15},{1,0},{2,1},{3,2},{4,3},{5,4},{6,5},{7,6},{8,7},{9,8},{10,9... | collective-permute-start | bytes 786440 | tf_op jit(solution)/shard_map/ppermute | solution.py:24
  77.5 2.4 collective-permute-done
  81.8 5.1 %collective-permute-start.3 = (bf16[128,1024]{1,0:T(8,128)(2,1)S(1)}, bf16[128,1024]{1,0:T(8,128)(2,1)S(1)}, u32[]{:S(2)}, u32[]{:S(2)}) collective-permute-start(bf16[128,1024]{1,0:T(8,128)(2,1)S(1)} %collective-permute-done.1), channel_id=1, source_target_pairs={{0,15},{1,0},{2,1},{3,2},{4,3},{5,4},{6,5},{7,6},{8,7},{9,8},{10,9... | collective-permute-start | bytes 786440 | tf_op jit(solution)/shard_map/ppermute | solution.py:24
  91.3 5.1 %collective-permute-start.5 = (bf16[128,1024]{1,0:T(8,128)(2,1)S(1)}, bf16[128,1024]{1,0:T(8,128)(2,1)S(1)}, u32[]{:S(2)}, u32[]{:S(2)}) collective-permute-start(bf16[128,1024]{1,0:T(8,128)(2,1)S(1)} %collective-permute-done.3), channel_id=1, source_target_pairs={{0,15},{1,0},{2,1},{3,2},{4,3},{5,4},{6,5},{7,6},{8,7},{9,8},{10,9... | collective-permute-start | bytes 786440 | tf_op jit(solution)/shard_map/ppermute | solution.py:24
  100.7 24.8 %all_gather.11 = bf16[128,1024]{0,1:T(8,128)(2,1)S(1)} all-gather(bf16[128,32]{0,1:T(8,128)(2,1)S(1)} %copy-done.1), channel_id=1, replica_groups=mesh['dp'=32,'tm'=16] {'dp'}, dimensions={1}, use_global_device_ids=true | all-gather | bytes 270336 | tf_op jit(solution)/shard_map/all_gather | solution.py:60
  126.2 5.2 %collective-permute-start.7 = (bf16[128,1024]{1,0:T(8,128)(2,1)S(1)}, bf16[128,1024]{1,0:T(8,128)(2,1)S(1)}, u32[]{:S(2)}, u32[]{:S(2)}) collective-permute-start(bf16[128,1024]{1,0:T(8,128)(2,1)S(1)} %collective-permute-done.5), channel_id=1, source_target_pairs={{0,15},{1,0},{2,1},{3,2},{4,3},{5,4},{6,5},{7,6},{8,7},{9,8},{10,9... | collective-permute-start | bytes 786440 | tf_op jit(solution)/shard_map/ppermute | solution.py:24
  137.7 5.6 %collective-permute-start.9 = (bf16[128,1024]{1,0:T(8,128)(2,1)S(1)}, bf16[128,1024]{1,0:T(8,128)(2,1)S(1)}, u32[]{:S(2)}, u32[]{:S(2)}) collective-permute-start(bf16[128,1024]{1,0:T(8,128)(2,1)S(1)} %collective-permute-done.7), channel_id=1, source_target_pairs={{0,15},{1,0},{2,1},{3,2},{4,3},{5,4},{6,5},{7,6},{8,7},{9,8},{10,9... | collective-permute-start | bytes 786440 | tf_op jit(solution)/shard_map/ppermute | solution.py:24
  148.8 5.6 %collective-permute-start.11 = (bf16[128,1024]{1,0:T(8,128)(2,1)S(1)}, bf16[128,1024]{1,0:T(8,128)(2,1)S(1)}, u32[]{:S(2)}, u32[]{:S(2)}) collective-permute-start(bf16[128,1024]{1,0:T(8,128)(2,1)S(1)} %collective-permute-done.9), channel_id=1, source_target_pairs={{0,15},{1,0},{2,1},{3,2},{4,3},{5,4},{6,5},{7,6},{8,7},{9,8},{10,9... | collective-permute-start | bytes 786440 | tf_op jit(solution)/shard_map/ppermute | solution.py:24
  159.0 5.6 %collective-permute-start.13 = (bf16[128,1024]{1,0:T(8,128)(2,1)S(1)}, bf16[128,1024]{1,0:T(8,128)(2,1)S(1)}, u32[]{:S(2)}, u32[]{:S(2)}) collective-permute-start(bf16[128,1024]{1,0:T(8,128)(2,1)S(1)} %collective-permute-done.11), channel_id=1, source_target_pairs={{0,15},{1,0},{2,1},{3,2},{4,3},{5,4},{6,5},{7,6},{8,7},{9,8},{10,9... | collective-permute-start | bytes 786440 | tf_op jit(solution)/shard_map/ppermute | solution.py:24
  169.7 5.2 %collective-permute-done.14 = bf16[128,1024]{1,0:T(8,128)(2,1)S(1)} collective-permute-done((bf16[128,1024]{1,0:T(8,128)(2,1)S(1)}, bf16[128,1024]{1,0:T(8,128)(2,1)S(1)}, u32[]{:S(2)}, u32[]{:S(2)}) %collective-permute-start.14) | collective-permute-done | bytes 262176 | tf_op jit(solution)/shard_map/ppermute | solution.py:19
  175.6 3.5 %fusion.12 = f32[2048,128]{1,0:T(8,128)S(1)} fusion(bf16[2048,1024]{1,0:T(8,128)(2,1)} %constant_dynamic-update-slice_fusion, bf16[9,1024,128]{2,1,0:T(8,128)(2,1)S(1)} %copy-done), kind=kOutput, calls=%fused_computation.12 | convolution fusion | flops 536870912 | bytes 5505024 | tf_op jit(solution)/shard_map/dot_general | solution.py:54
  179.0 4.4 %fusion.10 = f32[2048,128]{1,0:T(8,128)} fusion(bf16[2048,1024]{1,0:T(8,128)(2,1)} %constant_dynamic-update-slice_fusion, bf16[9,1024,128]{2,1,0:T(8,128)(2,1)S(1)} %copy-done), kind=kOutput, calls=%fused_computation.10 | convolution fusion | flops 536870912 | bytes 5505024 | tf_op jit(solution)/shard_map/dot_general | solution.py:54
  183.5 4.5 %fusion.8 = f32[2048,128]{1,0:T(8,128)} fusion(bf16[2048,1024]{1,0:T(8,128)(2,1)} %constant_dynamic-update-slice_fusion, bf16[9,1024,128]{2,1,0:T(8,128)(2,1)S(1)} %copy-done), kind=kOutput, calls=%fused_computation.8 | convolution fusion | flops 536870912 | bytes 5505024 | tf_op jit(solution)/shard_map/dot_general | solution.py:54
  188.0 4.4 %fusion.6 = f32[2048,128]{1,0:T(8,128)} fusion(bf16[2048,1024]{1,0:T(8,128)(2,1)} %constant_dynamic-update-slice_fusion, bf16[9,1024,128]{2,1,0:T(8,128)(2,1)S(1)} %copy-done), kind=kOutput, calls=%fused_computation.6 | convolution fusion | flops 536870912 | bytes 5505024 | tf_op jit(solution)/shard_map/dot_general | solution.py:54
  192.4 4.4 %fusion.4 = f32[2048,128]{1,0:T(8,128)} fusion(bf16[2048,1024]{1,0:T(8,128)(2,1)} %constant_dynamic-update-slice_fusion, bf16[9,1024,128]{2,1,0:T(8,128)(2,1)S(1)} %copy-done), kind=kOutput, calls=%fused_computation.4 | convolution fusion | flops 536870912 | bytes 5505024 | tf_op jit(solution)/shard_map/dot_general | solution.py:54
  196.9 4.4 %fusion.2 = f32[2048,128]{1,0:T(8,128)} fusion(bf16[2048,1024]{1,0:T(8,128)(2,1)} %constant_dynamic-update-slice_fusion, bf16[9,1024,128]{2,1,0:T(8,128)(2,1)S(1)} %copy-done), kind=kOutput, calls=%fused_computation.2 | convolution fusion | flops 536870912 | bytes 5505024 | tf_op jit(solution)/shard_map/dot_general | solution.py:54
  201.3 4.5 %fusion = f32[2048,128]{1,0:T(8,128)} fusion(bf16[2048,1024]{1,0:T(8,128)(2,1)} %constant_dynamic-update-slice_fusion, bf16[9,1024,128]{2,1,0:T(8,128)(2,1)S(1)} %copy-done), kind=kOutput, calls=%fused_computation | convolution fusion | flops 536870912 | bytes 5505024 | tf_op jit(solution)/shard_map/dot_general | solution.py:54
  205.8 3.4 %fusion.66 = f32[2048,128]{1,0:T(8,128)S(1)} fusion(bf16[2048,1024]{1,0:T(8,128)(2,1)} %constant_dynamic-update-slice_fusion, bf16[9,1024,128]{2,1,0:T(8,128)(2,1)S(1)} %copy-done), kind=kOutput, calls=%fused_computation.48 | convolution fusion | flops 536870912 | bytes 5505024 | tf_op jit(solution)/shard_map/dot_general | solution.py:54
  209.2 8.6 %convolution_convert_fusion = bf16[2048,1024]{1,0:T(8,128)(2,1)} fusion(bf16[128,1024]{0,1:T(8,128)(2,1)S(1)} %all_gather.11, f32[2048,128]{1,0:T(8,128)} %fusion, f32[2048,128]{1,0:T(8,128)} %fusion.2, f32[2048,128]{1,0:T(8,128)} %fusion.4, f32[2048,128]{1,0:T(8,128)} %fusion.6, f32[2048,128]{1,0:T(8,128)S(1)} %fusion.66, f32[2048,128]{1,0:T(8,128)} %fusion.8, ...), kind=kOutput, calls=%fused_computation.16 | convolution fusion | flops 1078460416 | bytes 17301504 | tf_op jit(solution)/shard_map/dot_general | solution.py:62
  217.9 75.6 %reduce-scatter.2.cloned.1.call-done = bf16[128,1024]{1,0:T(8,128)(2,1)} async-done(((bf16[2048,1024]{1,0:T(8,128)(2,1)}), bf16[128,1024]{1,0:T(8,128)(2,1)}) %reduce-scatter.2.cloned.1.call-update) | async-done | bytes 262160 | tf_op jit(solution)/shard_map/reduce_scatter | solution.py:61
  (60 shorter events, 41.1 us)
Async XLA Ops:
  6.5 94.2 %copy-start.1 = (bf16[128,32]{0,1:T(8,128)(2,1)S(1)}, bf16[128,32]{0,1:T(8,128)(2,1)}, u32[]{:S(2)}) copy-start(bf16[128,32]{0,1:T(8,128)(2,1)} %param.8) | copy-start | bytes 24580
  6.5 287.0 %reduce-scatter.2.cloned.1.call-start = ((), (), s32[]{:S(2)}) async-start(), calls=%async_computation.1 | async-start | bytes 4456448 | tf_op jit(solution)/shard_map/reduce_scatter | solution.py:61
  70.4 9.5 %collective-permute-start = (bf16[128,1024]{1,0:T(8,128)(2,1)S(1)}, bf16[128,1024]{1,0:T(8,128)(2,1)S(1)}, u32[]{:S(2)}, u32[]{:S(2)}) collective-permute-start(bf16[128,1024]{1,0:T(8,128)(2,1)S(1)} %get-tuple-element.6), channel_id=1, source_target_pairs={{0,1},{1,2},{2,3},{3,4},{4,5},{5,6},{6,7},{7,8},{8,9},{9,10},{10,1... | collective-permute-start | bytes 786440 | tf_op jit(solution)/shard_map/ppermute | solution.py:19
  73.4 8.4 %collective-permute-start.1 = (bf16[128,1024]{1,0:T(8,128)(2,1)S(1)}, bf16[128,1024]{1,0:T(8,128)(2,1)S(1)}, u32[]{:S(2)}, u32[]{:S(2)}) collective-permute-start(bf16[128,1024]{1,0:T(8,128)(2,1)S(1)} %get-tuple-element.6), channel_id=1, source_target_pairs={{0,15},{1,0},{2,1},{3,2},{4,3},{5,4},{6,5},{7,6},{8,7},{9,8},{10,9... | collective-permute-start | bytes 786440 | tf_op jit(solution)/shard_map/ppermute | solution.py:24
  79.9 9.5 %collective-permute-start.2 = (bf16[128,1024]{1,0:T(8,128)(2,1)S(1)}, bf16[128,1024]{1,0:T(8,128)(2,1)S(1)}, u32[]{:S(2)}, u32[]{:S(2)}) collective-permute-start(bf16[128,1024]{1,0:T(8,128)(2,1)S(1)} %collective-permute-done), channel_id=1, source_target_pairs={{0,1},{1,2},{2,3},{3,4},{4,5},{5,6},{6,7},{7,8},{8,9},{9,10},{10,1... | collective-permute-start | bytes 786440 | tf_op jit(solution)/shard_map/ppermute | solution.py:19
  81.8 9.5 %collective-permute-start.3 = (bf16[128,1024]{1,0:T(8,128)(2,1)S(1)}, bf16[128,1024]{1,0:T(8,128)(2,1)S(1)}, u32[]{:S(2)}, u32[]{:S(2)}) collective-permute-start(bf16[128,1024]{1,0:T(8,128)(2,1)S(1)} %collective-permute-done.1), channel_id=1, source_target_pairs={{0,15},{1,0},{2,1},{3,2},{4,3},{5,4},{6,5},{7,6},{8,7},{9,8},{10,9... | collective-permute-start | bytes 786440 | tf_op jit(solution)/shard_map/ppermute | solution.py:24
  89.4 9.5 %collective-permute-start.4 = (bf16[128,1024]{1,0:T(8,128)(2,1)S(1)}, bf16[128,1024]{1,0:T(8,128)(2,1)S(1)}, u32[]{:S(2)}, u32[]{:S(2)}) collective-permute-start(bf16[128,1024]{1,0:T(8,128)(2,1)S(1)} %collective-permute-done.2), channel_id=1, source_target_pairs={{0,1},{1,2},{2,3},{3,4},{4,5},{5,6},{6,7},{7,8},{8,9},{9,10},{10,1... | collective-permute-start | bytes 786440 | tf_op jit(solution)/shard_map/ppermute | solution.py:19
  91.3 35.0 %collective-permute-start.5 = (bf16[128,1024]{1,0:T(8,128)(2,1)S(1)}, bf16[128,1024]{1,0:T(8,128)(2,1)S(1)}, u32[]{:S(2)}, u32[]{:S(2)}) collective-permute-start(bf16[128,1024]{1,0:T(8,128)(2,1)S(1)} %collective-permute-done.3), channel_id=1, source_target_pairs={{0,15},{1,0},{2,1},{3,2},{4,3},{5,4},{6,5},{7,6},{8,7},{9,8},{10,9... | collective-permute-start | bytes 786440 | tf_op jit(solution)/shard_map/ppermute | solution.py:24
  98.8 33.4 %collective-permute-start.6 = (bf16[128,1024]{1,0:T(8,128)(2,1)S(1)}, bf16[128,1024]{1,0:T(8,128)(2,1)S(1)}, u32[]{:S(2)}, u32[]{:S(2)}) collective-permute-start(bf16[128,1024]{1,0:T(8,128)(2,1)S(1)} %collective-permute-done.4), channel_id=1, source_target_pairs={{0,1},{1,2},{2,3},{3,4},{4,5},{5,6},{6,7},{7,8},{8,9},{9,10},{10,1... | collective-permute-start | bytes 786440 | tf_op jit(solution)/shard_map/ppermute | solution.py:19
  125.5 50.1 %copy-start = (bf16[9,1024,128]{2,1,0:T(8,128)(2,1)S(1)}, bf16[9,1024,128]{2,1,0:T(8,128)(2,1)}, u32[]{:S(2)}) copy-start(bf16[9,1024,128]{2,1,0:T(8,128)(2,1)} %param.7) | copy-start | bytes 7077892
  126.2 11.5 %collective-permute-start.7 = (bf16[128,1024]{1,0:T(8,128)(2,1)S(1)}, bf16[128,1024]{1,0:T(8,128)(2,1)S(1)}, u32[]{:S(2)}, u32[]{:S(2)}) collective-permute-start(bf16[128,1024]{1,0:T(8,128)(2,1)S(1)} %collective-permute-done.5), channel_id=1, source_target_pairs={{0,15},{1,0},{2,1},{3,2},{4,3},{5,4},{6,5},{7,6},{8,7},{9,8},{10,9... | collective-permute-start | bytes 786440 | tf_op jit(solution)/shard_map/ppermute | solution.py:24
  132.2 11.8 %collective-permute-start.8 = (bf16[128,1024]{1,0:T(8,128)(2,1)S(1)}, bf16[128,1024]{1,0:T(8,128)(2,1)S(1)}, u32[]{:S(2)}, u32[]{:S(2)}) collective-permute-start(bf16[128,1024]{1,0:T(8,128)(2,1)S(1)} %collective-permute-done.6), channel_id=1, source_target_pairs={{0,1},{1,2},{2,3},{3,4},{4,5},{5,6},{6,7},{7,8},{8,9},{9,10},{10,1... | collective-permute-start | bytes 786440 | tf_op jit(solution)/shard_map/ppermute | solution.py:19
  137.7 11.1 %collective-permute-start.9 = (bf16[128,1024]{1,0:T(8,128)(2,1)S(1)}, bf16[128,1024]{1,0:T(8,128)(2,1)S(1)}, u32[]{:S(2)}, u32[]{:S(2)}) collective-permute-start(bf16[128,1024]{1,0:T(8,128)(2,1)S(1)} %collective-permute-done.7), channel_id=1, source_target_pairs={{0,15},{1,0},{2,1},{3,2},{4,3},{5,4},{6,5},{7,6},{8,7},{9,8},{10,9... | collective-permute-start | bytes 786440 | tf_op jit(solution)/shard_map/ppermute | solution.py:24
  144.1 11.1 %collective-permute-start.10 = (bf16[128,1024]{1,0:T(8,128)(2,1)S(1)}, bf16[128,1024]{1,0:T(8,128)(2,1)S(1)}, u32[]{:S(2)}, u32[]{:S(2)}) collective-permute-start(bf16[128,1024]{1,0:T(8,128)(2,1)S(1)} %collective-permute-done.8), channel_id=1, source_target_pairs={{0,1},{1,2},{2,3},{3,4},{4,5},{5,6},{6,7},{7,8},{8,9},{9,10},{10,1... | collective-permute-start | bytes 786440 | tf_op jit(solution)/shard_map/ppermute | solution.py:19
  148.8 10.2 %collective-permute-start.11 = (bf16[128,1024]{1,0:T(8,128)(2,1)S(1)}, bf16[128,1024]{1,0:T(8,128)(2,1)S(1)}, u32[]{:S(2)}, u32[]{:S(2)}) collective-permute-start(bf16[128,1024]{1,0:T(8,128)(2,1)S(1)} %collective-permute-done.9), channel_id=1, source_target_pairs={{0,15},{1,0},{2,1},{3,2},{4,3},{5,4},{6,5},{7,6},{8,7},{9,8},{10,9... | collective-permute-start | bytes 786440 | tf_op jit(solution)/shard_map/ppermute | solution.py:24
  155.1 10.2 %collective-permute-start.12 = (bf16[128,1024]{1,0:T(8,128)(2,1)S(1)}, bf16[128,1024]{1,0:T(8,128)(2,1)S(1)}, u32[]{:S(2)}, u32[]{:S(2)}) collective-permute-start(bf16[128,1024]{1,0:T(8,128)(2,1)S(1)} %collective-permute-done.10), channel_id=1, source_target_pairs={{0,1},{1,2},{2,3},{3,4},{4,5},{5,6},{6,7},{7,8},{8,9},{9,10},{10,1... | collective-permute-start | bytes 786440 | tf_op jit(solution)/shard_map/ppermute | solution.py:19
  159.0 9.9 %collective-permute-start.13 = (bf16[128,1024]{1,0:T(8,128)(2,1)S(1)}, bf16[128,1024]{1,0:T(8,128)(2,1)S(1)}, u32[]{:S(2)}, u32[]{:S(2)}) collective-permute-start(bf16[128,1024]{1,0:T(8,128)(2,1)S(1)} %collective-permute-done.11), channel_id=1, source_target_pairs={{0,15},{1,0},{2,1},{3,2},{4,3},{5,4},{6,5},{7,6},{8,7},{9,8},{10,9... | collective-permute-start | bytes 786440 | tf_op jit(solution)/shard_map/ppermute | solution.py:24
  165.4 9.5 %collective-permute-start.14 = (bf16[128,1024]{1,0:T(8,128)(2,1)S(1)}, bf16[128,1024]{1,0:T(8,128)(2,1)S(1)}, u32[]{:S(2)}, u32[]{:S(2)}) collective-permute-start(bf16[128,1024]{1,0:T(8,128)(2,1)S(1)} %collective-permute-done.12), channel_id=1, source_target_pairs={{0,1},{1,2},{2,3},{3,4},{4,5},{5,6},{6,7},{7,8},{8,9},{9,10},{10,1... | collective-permute-start | bytes 786440 | tf_op jit(solution)/shard_map/ppermute | solution.py:19
  217.9 77.9 %copy-start.2 = (f32[1024]{0:T(1024)S(1)}, f32[1024]{0:T(1024)}, u32[]{:S(2)}) copy-start(f32[1024]{0:T(1024)} %param.9) | copy-start | bytes 12292
Sparse Core Ops, SparseCore 0:
  218.0 75.4 reduce-scatter.1
